TPU v7x, 32 devices: a whole 2x2x4 slice. The times are simulated.
32 devices in a mesh: dom: 2 (over x), head: 16 (over z, y, core).
Axes of the slice: x: 2, y: 2, z: 4, core: 2. Of those that a mesh axis runs over, the one named last changes fastest.
Arguments:
- queries: bfloat16 [4096, 1024], P(('dom', 'head')), may hold values from -10 to 10
- key_vectors: bfloat16 [4096, 1024], P(('dom', 'head')), may hold values from -8 to 8
- value_vectors: bfloat16 [4096, 1024], P(('dom', 'head')), may hold values from -6 to 6
- block_lists: int32 [32, 12], replicated, may hold values from 0 to 31, as said below
- out_weight: bfloat16 [1024, 1024], replicated, may hold values from -0.1875 to 0.1875
Outputs:
- mixed: bfloat16 [4096, 1024], P(('dom', 'head'))
Inputs may be any that keep to these rules, and one draw needn't show every extreme that they name: `block_lists`: partition p holds blocks p * 16 to (p + 1) * 16 - 1. In row b the first 4 entries are distinct blocks of b's own partition, b itself among them; the other 8 are distinct blocks of other partitions. The expander entries of one partition's query blocks fill other partitions 128 entries at a time, so each other partition receives none, 128, or one remainder, and one receives exactly 128.
All inputs are finite; a program needn't handle non-finite values.
Results may differ from a plain program's by a relative error of at most 0.0051.
Values may be sent and summed in bfloat16 or wider, within the bound.
A program may use at most 64 MiB of HBM per device.

v0:
```python
import jax
import jax.numpy as jnp
from jax import lax
from jax.sharding import PartitionSpec as P

D = 1024
HEADS = 16
BLK = 128
LC = 4
LE = 8


lowest_value = -1e30


def from_behind(x, axis, by):
    devices = lax.axis_size(axis)
    return lax.ppermute(x, axis, [(i, (i + by) % devices) for i in range(devices)])


def attend(query_tiles, key_tiles, value_tiles, factor):
    tiles = key_tiles.shape[0]
    heads_dev = key_tiles.shape[2]
    head_dim = key_tiles.shape[3]
    listed_count = key_tiles.shape[1] // BLK
    key_parts = key_tiles.reshape(tiles, listed_count, BLK, heads_dev, head_dim)
    value_parts = value_tiles.reshape(tiles, listed_count, BLK, heads_dev, head_dim)
    scores = (
        jnp.einsum("tqhd,tlkhd->tqhlk", query_tiles, key_parts, preferred_element_type=jnp.float32)
        * factor
    )
    block_high = jnp.max(scores, axis=-1)
    highest = jnp.max(block_high, axis=-1)
    scale_back = jnp.exp(block_high - highest[..., None])
    weights = jnp.exp(scores - block_high[..., None])
    totals = jnp.sum(scale_back * jnp.sum(weights, axis=-1), axis=-1)
    per_block = jnp.einsum(
        "tqhlk,tlkhd->tqhld",
        weights.astype(jnp.bfloat16),
        value_parts,
        preferred_element_type=jnp.float32,
    )
    summed = jnp.sum(per_block * scale_back[..., None], axis=3)
    return (summed, highest, totals)


def near_pass(query_blocks, key_blocks, value_blocks, near_ids, factor):
    blocks, block_rows, heads_dev, head_dim = query_blocks.shape
    groups = blocks // 4

    def group_pass(operands):
        query_group, id_group = operands
        key_group = key_blocks[id_group].reshape(4, -1, heads_dev, head_dim)
        value_group = value_blocks[id_group].reshape(4, -1, heads_dev, head_dim)
        return attend(query_group, key_group, value_group, factor)

    summed, highest, totals = lax.map(
        group_pass,
        (
            query_blocks.reshape(groups, 4, block_rows, heads_dev, head_dim),
            near_ids.reshape(groups, 4, -1),
        ),
    )
    return (
        summed.reshape(blocks, block_rows, heads_dev, head_dim),
        highest.reshape(blocks, block_rows, heads_dev),
        totals.reshape(blocks, block_rows, heads_dev),
    )


def slot_table(listed, wanted, capacity):
    places = jnp.cumsum(wanted.astype(jnp.int32)) - 1
    tile_slots = jnp.arange(capacity, dtype=jnp.int32)
    taking = wanted[None, :] & (places[None, :] == tile_slots[:, None])
    filled = jnp.any(taking, axis=1)
    entries = jnp.arange(listed.shape[0], dtype=jnp.int32)
    chosen_entry = jnp.sum(jnp.where(taking, entries[None, :], 0), axis=1)
    chosen_block = jnp.sum(jnp.where(taking, listed[None, :], 0), axis=1)
    return (filled, chosen_entry, chosen_block)


def merge_tiles(running, tile_query, filled, tile_summed, tile_highest, tile_totals):
    summed, highest, totals = running
    blocks = summed.shape[0]
    member = (tile_query[None, :] == jnp.arange(blocks, dtype=jnp.int32)[:, None]) & filled[None, :]
    reached = jnp.max(jnp.where(member[:, :, None, None], tile_highest[None], lowest_value), axis=1)
    new_highest = jnp.maximum(highest, reached)
    rescale = jnp.where(filled[:, None, None], jnp.exp(tile_highest - new_highest[tile_query]), 0.0)
    retain = jnp.exp(highest - new_highest)
    member_float = member.astype(jnp.float32)
    totals = totals * retain + jnp.einsum(
        "qt,tbh->qbh", member_float, rescale * tile_totals, precision=lax.Precision.HIGHEST
    )
    summed = summed * retain[..., None] + jnp.einsum(
        "qt,tbhd->qbhd",
        member_float,
        rescale[..., None] * tile_summed,
        precision=lax.Precision.HIGHEST,
    )
    return (summed, new_highest, totals)


def absorb(running, query_blocks, far_ids, key_blocks, value_blocks, first_block, capacity, factor):
    reach_blocks = key_blocks.shape[0]
    listed = far_ids.reshape(-1)
    wanted = (listed >= first_block) & (listed < first_block + reach_blocks)
    filled, chosen_entry, chosen_block = slot_table(listed, wanted, capacity)
    tile_query = chosen_entry // far_ids.shape[1]
    tile_key = jnp.where(filled, chosen_block - first_block, 0)
    tile_summed, tile_highest, tile_totals = attend(
        query_blocks[tile_query], key_blocks[tile_key], value_blocks[tile_key], factor
    )
    return merge_tiles(running, tile_query, filled, tile_summed, tile_highest, tile_totals)


def shards(queries, key_vectors, value_vectors, block_lists, out_weight):
    node_rows = queries.shape[0]
    head_dim = D // HEADS
    head_devices = lax.axis_size("head")
    row_split = max(1, head_devices // HEADS)
    groups = head_devices // row_split
    heads_dev = HEADS // groups
    head_cols = heads_dev * head_dim
    local_blocks = node_rows // BLK
    sub_rows = BLK // row_split
    query_parts = (
        queries.reshape(local_blocks, row_split, sub_rows, groups, head_cols)
        .transpose(0, 2, 3, 1, 4)
        .reshape(local_blocks * sub_rows, groups * row_split, head_cols)
    )

    def spread(tensor):
        return jnp.broadcast_to(
            tensor.reshape(node_rows, groups, 1, head_cols),
            (node_rows, groups, row_split, head_cols),
        ).reshape(node_rows, groups * row_split, head_cols)

    part_queries, part_keys, part_values = (
        lax.all_to_all(query_parts, "head", split_axis=1, concat_axis=0, tiled=True),
        lax.all_to_all(spread(key_vectors), "head", split_axis=1, concat_axis=0, tiled=True),
        lax.all_to_all(spread(value_vectors), "head", split_axis=1, concat_axis=0, tiled=True),
    )
    blocks = part_keys.shape[0] // BLK
    query_blocks = part_queries.reshape(blocks, sub_rows, heads_dev, head_dim)
    key_blocks = part_keys.reshape(blocks, BLK, heads_dev, head_dim)
    value_blocks = part_values.reshape(blocks, BLK, heads_dev, head_dim)
    domains = lax.axis_size("dom")
    domain_here = lax.axis_index("dom")
    score_factor = head_dim ** (-0.5)
    own_rows = lax.dynamic_slice_in_dim(block_lists, domain_here * blocks, blocks, 0)
    near_ids = own_rows[:, :LC] - domain_here * blocks
    fold_width = min(8, domains - 1)
    capacity = (blocks * LE + fold_width - 1) // fold_width
    running = near_pass(query_blocks, key_blocks, value_blocks, near_ids, score_factor)

    def visit_turn(stride, loop_state):
        visitors, partial_value = loop_state
        visitors = from_behind(visitors, "dom", 1)
        partial_value = from_behind(
            (partial_value[0], partial_value[1], partial_value[2]), "dom", 1
        )
        source = (domain_here - stride) % domains
        far_rows = lax.dynamic_slice_in_dim(block_lists, source * blocks, blocks, 0)[:, LC:]
        partial_value = absorb(
            partial_value,
            visitors,
            far_rows,
            key_blocks,
            value_blocks,
            domain_here * blocks,
            capacity,
            score_factor,
        )
        return (visitors, partial_value)

    carried = lax.fori_loop(1, domains, visit_turn, (query_blocks, running))
    running = from_behind(carried[1], "dom", 1)
    summed, highest, totals = running
    attended = (
        (summed / totals[..., None]).astype(jnp.bfloat16).reshape(blocks * sub_rows, 1, head_cols)
    )
    regrouped = lax.all_to_all(attended, "head", split_axis=0, concat_axis=1, tiled=True)
    restored = (
        regrouped.reshape(local_blocks, sub_rows, groups, row_split, head_cols)
        .transpose(0, 3, 1, 2, 4)
        .reshape(node_rows, D)
    )
    return jnp.dot(restored, out_weight, preferred_element_type=jnp.float32).astype(jnp.bfloat16)


def solution(mesh):
    in_specs = (
        P(("dom", "head"), None),
        P(("dom", "head"), None),
        P(("dom", "head"), None),
        P(),
        P(),
    )
    out_specs = P(("dom", "head"), None)
    return jax.shard_map(shards, mesh=mesh, in_specs=in_specs, out_specs=out_specs, check_vma=False)
```

profile of v0, /device:TPU:0, one launch (start us, length us, event | category | flops | bytes accessed | tf_op | source)
XLA Modules:
  0.0 137.8 jit_solution(9657936267287681404)
XLA Ops:
  0.0 1.9 %copy.93 = bf16[128,1024]{0,1:T(8,128)(2,1)} copy(bf16[128,1024]{1,0:T(8,128)(2,1)} %param.8) | data formatting | bytes 524288 | tf_op args[1]
  1.9 7.4 %all-to-all-start.1 = ((bf16[128,16,64]{0,2,1:T(8,128)(2,1)}), bf16[128,16,64]{0,2,1:T(8,128)(2,1)S(1)}, u32[]{:S(2)}, u32[]{:S(2)}) async-start(bf16[128,16,64]{0,2,1:T(8,128)(2,1)} %bitcast.22), calls=%async_computation.1 | async-start | bytes 524288 | tf_op jit(solution)/shard_map/all_to_all | solution.py:140
  10.8 1.8 %copy.94 = bf16[128,1024]{0,1:T(8,128)(2,1)} copy(bf16[128,1024]{1,0:T(8,128)(2,1)} %param.7) | data formatting | bytes 524288 | tf_op args[0]
  12.8 6.6 %all-to-all-done.1 = bf16[128,16,64]{0,2,1:T(8,128)(2,1)S(1)} async-done(((bf16[128,16,64]{0,2,1:T(8,128)(2,1)}), bf16[128,16,64]{0,2,1:T(8,128)(2,1)S(1)}, u32[]{:S(2)}, u32[]{:S(2)}) %all-to-all-start.1) | async-done | bytes 262176 | tf_op jit(solution)/shard_map/all_to_all | solution.py:140
  19.4 4.2 %all-to-all-start.2 = ((bf16[128,16,64]{0,2,1:T(8,128)(2,1)}), bf16[128,16,64]{0,2,1:T(8,128)(2,1)}, u32[]{:S(2)}, u32[]{:S(2)}) async-start(bf16[128,16,64]{0,2,1:T(8,128)(2,1)} %bitcast.25), calls=%async_computation.2 | async-start | bytes 524288 | tf_op jit(solution)/shard_map/all_to_all | solution.py:139
  23.8 1.8 %copy.92 = bf16[128,1024]{0,1:T(8,128)(2,1)} copy(bf16[128,1024]{1,0:T(8,128)(2,1)} %param.9) | data formatting | bytes 524288 | tf_op args[2]
  25.9 7.8 %all-to-all-done.2 = bf16[128,16,64]{0,2,1:T(8,128)(2,1)} async-done(((bf16[128,16,64]{0,2,1:T(8,128)(2,1)}), bf16[128,16,64]{0,2,1:T(8,128)(2,1)}, u32[]{:S(2)}, u32[]{:S(2)}) %all-to-all-start.2) | async-done | bytes 262176 | tf_op jit(solution)/shard_map/all_to_all | solution.py:139
  33.6 4.2 %all-to-all-start = ((bf16[128,16,64]{0,2,1:T(8,128)(2,1)}), bf16[128,16,64]{0,2,1:T(8,128)(2,1)}, u32[]{:S(2)}, u32[]{:S(2)}) async-start(bf16[128,16,64]{0,2,1:T(8,128)(2,1)} %bitcast.19), calls=%async_computation | async-start | bytes 524288 | tf_op jit(solution)/shard_map/all_to_all | solution.py:141
  38.7 1.6 %collective-permute-start.2 = (bf16[16,128,1,64]{1,3,0,2:T(8,128)(2,1)}, bf16[16,128,1,64]{1,3,0,2:T(8,128)(2,1)}, u32[]{:S(2)}, u32[]{:S(2)}) collective-permute-start(bf16[16,128,1,64]{1,3,0,2:T(8,128)(2,1)} %bitcast.27), channel_id=1, source_target_pairs={{0,16},{16,0},{1,17},{17,1},{2,18},{18,2},{3,19},{19,3},{4,20},{20... | collective-permute-start | bytes 786440 | tf_op jit(solution)/shard_map/while/body/eval_jaxpr/ppermute | solution.py:18
  40.3 7.6 %all-to-all-done = bf16[128,16,64]{0,2,1:T(8,128)(2,1)} async-done(((bf16[128,16,64]{0,2,1:T(8,128)(2,1)}), bf16[128,16,64]{0,2,1:T(8,128)(2,1)}, u32[]{:S(2)}, u32[]{:S(2)}) %all-to-all-start) | async-done | bytes 262176 | tf_op jit(solution)/shard_map/all_to_all | solution.py:141
  47.9 28.8 %while.2 = (s32[]{:T(128)}, f32[4,4,128,1,64]{2,1,0,4,3:T(4,128)}, f32[4,4,128,1]{2,1,3,0:T(4,128)S(1)}, f32[4,4,128,1]{2,3,1,0:T(1,128)S(1)}, s32[4,4,4]{2,1,0:...) while((s32[]{:T(128)}, f32[4,4,128,1,64]{2,1,0,4,3:T(4,128)}, ...), condition=%wide.region_6.7_spmd, body=%wide.region_0.6_spmd.sunk | while | flops 69175344 | bytes 5262889 | solution.py:57
  48.0 1.3 gather_fusion.1
  49.3 1.3 fusion.66
  50.8 2.2 %gather_fusion = bf16[16,128,64]{1,2,0:T(8,128)(2,1)} fusion(bf16[16,128,64]{1,2,0:T(8,128)(2,1)} %bitcast.162, s32[1024]{0:T(1024)S(1)} %pad_clamp_fusion.4), kind=kCustom, calls=%fused_computation.clone.1 | custom fusion | bytes 524352 | tf_op jit(solution)/shard_map/while/body/eval_jaxpr/gather | solution.py:54
  56.5 1.3 fusion.66
  58.0 2.2 %gather_fusion = bf16[16,128,64]{1,2,0:T(8,128)(2,1)} fusion(bf16[16,128,64]{1,2,0:T(8,128)(2,1)} %bitcast.162, s32[1024]{0:T(1024)S(1)} %pad_clamp_fusion.4), kind=kCustom, calls=%fused_computation.clone.1 | custom fusion | bytes 524352 | tf_op jit(solution)/shard_map/while/body/eval_jaxpr/gather | solution.py:54
  63.6 1.3 fusion.66
  65.2 2.2 %gather_fusion = bf16[16,128,64]{1,2,0:T(8,128)(2,1)} fusion(bf16[16,128,64]{1,2,0:T(8,128)(2,1)} %bitcast.162, s32[1024]{0:T(1024)S(1)} %pad_clamp_fusion.4), kind=kCustom, calls=%fused_computation.clone.1 | custom fusion | bytes 524352 | tf_op jit(solution)/shard_map/while/body/eval_jaxpr/gather | solution.py:54
  70.9 1.3 fusion.66
  72.4 2.2 %gather_fusion = bf16[16,128,64]{1,2,0:T(8,128)(2,1)} fusion(bf16[16,128,64]{1,2,0:T(8,128)(2,1)} %bitcast.162, s32[1024]{0:T(1024)S(1)} %pad_clamp_fusion.4), kind=kCustom, calls=%fused_computation.clone.1 | custom fusion | bytes 524352 | tf_op jit(solution)/shard_map/while/body/eval_jaxpr/gather | solution.py:54
  76.7 1.5 %collective-permute-start.1 = (f32[16,128,1]{1,0,2:T(8,128)S(1)}, f32[16,128,1]{1,0,2:T(8,128)S(1)}, u32[]{:S(2)}, u32[]{:S(2)}) collective-permute-start(f32[16,128,1]{1,0,2:T(8,128)S(1)} %bitcast.182), channel_id=1, source_target_pairs={{0,16},{16,0},{1,17},{17,1},{2,18},{18,2},{3,19},{19,3},{4,20},{20... | collective-permute-start | bytes 24584 | tf_op jit(solution)/shard_map/while/body/eval_jaxpr/ppermute | solution.py:18
  78.7 2.1 %gather_fusion.2 = bf16[128,128,64]{1,2,0:T(8,128)(2,1)} fusion(bf16[16,128,64]{1,2,0:T(8,128)(2,1)S(1)} %bitcast.170, s32[1024]{0:T(1024)S(1)} %pad_clamp_fusion.2), kind=kCustom, calls=%fused_computation.2 | custom fusion | bytes 4194816 | tf_op jit(solution)/shard_map/while/body/eval_jaxpr/gather | solution.py:111
  80.8 3.2 %gather_fusion.5 = bf16[128,128,64]{1,2,0:T(8,128)(2,1)} fusion(bf16[16,128,64]{1,2,0:T(8,128)(2,1)} %bitcast.45, s32[1024]{0:T(1024)S(1)} %pad_clamp_fusion.2), kind=kCustom, calls=%fused_computation.5 | custom fusion | bytes 4194816 | tf_op jit(solution)/shard_map/while/body/eval_jaxpr/gather | solution.py:111
  84.0 1.5 %collective-permute-start = (f32[16,128,1,64]{1,0,3,2:T(8,128)S(1)}, f32[16,128,1,64]{1,0,3,2:T(8,128)S(1)}, u32[]{:S(2)}, u32[]{:S(2)}) collective-permute-start(f32[16,128,1,64]{1,0,3,2:T(8,128)S(1)} %bitcast.186), channel_id=1, source_target_pairs={{0,16},{16,0},{1,17},{17,1},{2,18},{18,2},{3,19},{19,3},{4,20},{20... | collective-permute-start | bytes 1572872 | tf_op jit(solution)/shard_map/while/body/eval_jaxpr/ppermute | solution.py:18
  85.5 3.1 %gather_fusion.3 = bf16[128,128,64]{1,2,0:T(8,128)(2,1)} fusion(bf16[16,128,64]{1,2,0:T(8,128)(2,1)} %bitcast.36, s32[1024]{0:T(1024)S(1)} %pad_clamp_fusion.1), kind=kCustom, calls=%fused_computation.3 | custom fusion | bytes 4194816 | tf_op jit(solution)/shard_map/while/body/eval_jaxpr/gather | solution.py:111
  88.6 7.0 %bitcast_reduce_fusion = (f32[128,128]{1,0:T(8,128)S(1)}, f32[128,128,128]{2,1,0:T(8,128)}) fusion(bf16[128,128,64]{1,2,0:T(8,128)(2,1)} %gather_fusion.2, bf16[128,128,64]{1,2,0:T(8,128)(2,1)} %gather_fusion.3), kind=kOutput, calls=%fused_computation.27 | convolution fusion | flops 272613376 | bytes 12648448 | tf_op jit(solution)/shard_map/while/body/eval_jaxpr/tqhd,tlkhd->tqhlk/dot_general | solution.py:29
  96.7 6.3 %bitcast_multiply_fusion = f32[128,128,64]{1,2,0:T(8,128)S(1)} fusion(bf16[128,128,64]{1,2,0:T(8,128)(2,1)} %gather_fusion.5, f32[128,128,128]{2,1,0:T(8,128)} %get-tuple-element.153, f32[128,128]{1,0:T(8,128)S(1)} %get-tuple-element.152, f32[128,128]{1,0:T(8,128)S(1)} %get-tuple-element.149, f32[128,128]{1,0:T(8,128)S(1)} %get-tuple-element.148), kind=kOutput, calls=%fused_computation.33 | convolution fusion | flops 276824064 | bytes 14876672 | tf_op jit(solution)/shard_map/while/body/eval_jaxpr/tqhlk,tlkhd->tqhld/dot_general | solution.py:37
  103.1 3.9 %multiply_add_fusion = f32[16,128,1,64]{1,0,3,2:T(8,128)S(1)} fusion(f32[16,128,1,64]{1,0,3,2:T(8,128)S(1)} %collective-permute-done, f32[16,128]{1,0:T(8,128)S(1)} %get-tuple-element.151, f32[128,128,64]{1,2,0:T(8,128)S(1)} %bitcast_multiply_fusion, s32[128]{0:T(128)S(1)} %and_select_fusion, pred[128]{0:T(512)(128)(4,1)S(1)} %fusion.32), kind=kOutput, calls=%fused_computation.44 | convolution fusion | flops 201592832 | bytes 5251712 | tf_op jit(solution)/shard_map/while/body/eval_jaxpr/qt,tbhd->qbhd/dot_general | solution.py:94
  107.6 2.8 %fusion.12 = f32[128,128]{1,0:T(8,128)S(1)} fusion(f32[128,128,128]{2,1,0:T(8,128)S(1)} %bitcast.172, f32[128,128]{1,0:T(8,128)S(1)} %get-tuple-element.152), kind=kLoop, calls=%fused_computation.29 | loop fusion | flops 6275072 | bytes 8519680 | tf_op jit(solution)/shard_map/while/body/eval_jaxpr/reduce_sum | solution.py:36
  110.5 1.5 %collective-permute-start.5 = (f32[16,128,1]{1,0,2:T(8,128)S(1)}, f32[16,128,1]{1,0,2:T(8,128)S(1)}, u32[]{:S(2)}, u32[]{:S(2)}) collective-permute-start(f32[16,128,1]{1,0,2:T(8,128)S(1)} %multiply_add_fusion.1), channel_id=1, source_target_pairs={{0,16},{16,0},{1,17},{17,1},{2,18},{18,2},{3,19},{19,3},{4,20},{20... | collective-permute-start | bytes 24584 | tf_op jit(solution)/shard_map/ppermute | solution.py:18
  112.0 8.0 %collective-permute-done.5 = f32[16,128,1]{1,0,2:T(8,128)S(1)} collective-permute-done((f32[16,128,1]{1,0,2:T(8,128)S(1)}, f32[16,128,1]{1,0,2:T(8,128)S(1)}, u32[]{:S(2)}, u32[]{:S(2)}) %collective-permute-start.5) | collective-permute-done | bytes 8224 | tf_op jit(solution)/shard_map/ppermute | solution.py:18
  122.2 13.1 %all_to_all.60 = bf16[16,2,4096]{2,1,0:T(2,128)(2,1)S(1)} all-to-all(bf16[16,2,4096]{2,1,0:T(2,128)(2,1)S(1)} %reshape.525), channel_id=1, replica_groups=mesh['dom'=2,'head'=16] {'head'}, dimensions={0} | all-to-all | bytes 524288 | tf_op jit(solution)/shard_map/all_to_all | solution.py:182
  (95 shorter events, 23.2 us)
Async XLA Ops:
  0.0 136.7 %copy-start = (bf16[1024,1024]{1,0:T(8,128)(2,1)S(1)}, bf16[1024,1024]{1,0:T(8,128)(2,1)}, u32[]{:S(2)}) copy-start(bf16[1024,1024]{1,0:T(8,128)(2,1)} %param.11) | copy-start | bytes 6291460
  1.9 17.4 %all-to-all-start.1 = ((bf16[128,16,64]{0,2,1:T(8,128)(2,1)}), bf16[128,16,64]{0,2,1:T(8,128)(2,1)S(1)}, u32[]{:S(2)}, u32[]{:S(2)}) async-start(bf16[128,16,64]{0,2,1:T(8,128)(2,1)} %bitcast.22), calls=%async_computation.1 | async-start | bytes 524288 | tf_op jit(solution)/shard_map/all_to_all | solution.py:140
  19.4 14.2 %all-to-all-start.2 = ((bf16[128,16,64]{0,2,1:T(8,128)(2,1)}), bf16[128,16,64]{0,2,1:T(8,128)(2,1)}, u32[]{:S(2)}, u32[]{:S(2)}) async-start(bf16[128,16,64]{0,2,1:T(8,128)(2,1)} %bitcast.25), calls=%async_computation.2 | async-start | bytes 524288 | tf_op jit(solution)/shard_map/all_to_all | solution.py:139
  33.6 14.3 %all-to-all-start = ((bf16[128,16,64]{0,2,1:T(8,128)(2,1)}), bf16[128,16,64]{0,2,1:T(8,128)(2,1)}, u32[]{:S(2)}, u32[]{:S(2)}) async-start(bf16[128,16,64]{0,2,1:T(8,128)(2,1)} %bitcast.19), calls=%async_computation | async-start | bytes 524288 | tf_op jit(solution)/shard_map/all_to_all | solution.py:141
  38.7 46.8 %collective-permute-start.2 = (bf16[16,128,1,64]{1,3,0,2:T(8,128)(2,1)}, bf16[16,128,1,64]{1,3,0,2:T(8,128)(2,1)}, u32[]{:S(2)}, u32[]{:S(2)}) collective-permute-start(bf16[16,128,1,64]{1,3,0,2:T(8,128)(2,1)} %bitcast.27), channel_id=1, source_target_pairs={{0,16},{16,0},{1,17},{17,1},{2,18},{18,2},{3,19},{19,3},{4,20},{20... | collective-permute-start | bytes 786440 | tf_op jit(solution)/shard_map/while/body/eval_jaxpr/ppermute | solution.py:18
  76.7 19.3 %collective-permute-start.1 = (f32[16,128,1]{1,0,2:T(8,128)S(1)}, f32[16,128,1]{1,0,2:T(8,128)S(1)}, u32[]{:S(2)}, u32[]{:S(2)}) collective-permute-start(f32[16,128,1]{1,0,2:T(8,128)S(1)} %bitcast.182), channel_id=1, source_target_pairs={{0,16},{16,0},{1,17},{17,1},{2,18},{18,2},{3,19},{19,3},{4,20},{20... | collective-permute-start | bytes 24584 | tf_op jit(solution)/shard_map/while/body/eval_jaxpr/ppermute | solution.py:18
  78.2 32.2 %collective-permute-start.4 = (f32[16,128,1]{1,0,2:T(8,128)S(1)}, f32[16,128,1]{1,0,2:T(8,128)S(1)}, u32[]{:S(2)}, u32[]{:S(2)}) collective-permute-start(f32[16,128,1]{1,0,2:T(8,128)S(1)} %bitcast.184), channel_id=1, source_target_pairs={{0,16},{16,0},{1,17},{17,1},{2,18},{18,2},{3,19},{19,3},{4,20},{20... | collective-permute-start | bytes 24584 | tf_op jit(solution)/shard_map/while/body/eval_jaxpr/ppermute | solution.py:18
  80.8 3.2 %copy-start.1 = (f32[4,4,128,1,64]{2,1,0,4,3:T(4,128)S(1)}, f32[4,4,128,1,64]{2,1,0,4,3:T(4,128)}, u32[]{:S(2)}) copy-start(f32[4,4,128,1,64]{2,1,0,4,3:T(4,128)} %get-tuple-element.79) | copy-start | bytes 1572868
  84.0 19.1 %collective-permute-start = (f32[16,128,1,64]{1,0,3,2:T(8,128)S(1)}, f32[16,128,1,64]{1,0,3,2:T(8,128)S(1)}, u32[]{:S(2)}, u32[]{:S(2)}) collective-permute-start(f32[16,128,1,64]{1,0,3,2:T(8,128)S(1)} %bitcast.186), channel_id=1, source_target_pairs={{0,16},{16,0},{1,17},{17,1},{2,18},{18,2},{3,19},{19,3},{4,20},{20... | collective-permute-start | bytes 1572872 | tf_op jit(solution)/shard_map/while/body/eval_jaxpr/ppermute | solution.py:18
  96.7 10.8 %slice-start = ((s8[8388608]{0:T(1024)(128)(4,1)}), s8[4194304]{0:T(1024)(128)(4,1)S(1)}, s32[]{:S(2)}) async-start(s8[8388608]{0:T(1024)(128)(4,1)} %bitcast.171), calls=%async_computation.4 | async-start | bytes 8388608
  96.7 10.8 %slice-start.1 = ((s8[8388608]{0:T(1024)(128)(4,1)}), s8[4194304]{0:T(1024)(128)(4,1)S(1)}, s32[]{:S(2)}) async-start(s8[8388608]{0:T(1024)(128)(4,1)} %bitcast.171), calls=%async_computation.5 | async-start | bytes 8388608
  107.0 13.1 %collective-permute-start.3 = (f32[16,128,1,64]{1,0,3,2:T(8,128)S(1)}, f32[16,128,1,64]{1,0,3,2:T(8,128)S(1)}, u32[]{:S(2)}, u32[]{:S(2)}) collective-permute-start(f32[16,128,1,64]{1,0,3,2:T(8,128)S(1)} %multiply_add_fusion), channel_id=1, source_target_pairs={{0,16},{16,0},{1,17},{17,1},{2,18},{18,2},{3,19},{19,3},{4,20},{20... | collective-permute-start | bytes 1572872 | tf_op jit(solution)/shard_map/ppermute | solution.py:18
  110.5 9.5 %collective-permute-start.5 = (f32[16,128,1]{1,0,2:T(8,128)S(1)}, f32[16,128,1]{1,0,2:T(8,128)S(1)}, u32[]{:S(2)}, u32[]{:S(2)}) collective-permute-start(f32[16,128,1]{1,0,2:T(8,128)S(1)} %multiply_add_fusion.1), channel_id=1, source_target_pairs={{0,16},{16,0},{1,17},{17,1},{2,18},{18,2},{3,19},{19,3},{4,20},{20... | collective-permute-start | bytes 24584 | tf_op jit(solution)/shard_map/ppermute | solution.py:18
where the time goes:
time: 139 us; the launch traced here: 138 us
  local copies, waits for them, and re-layouts  35.4 us (25%)
  waiting for transfers between devices  30 us (22%)
  matrix products  28.7 us (21%)
  starting transfers between devices  23 us (17%)
  blocking collectives  13.1 us (9%)
  other arithmetic  7.3 us (5%)
    all_to_all x1, blocking collectives, shards(): lax.all_to_all(attended, 'head', split_axis=0, concat_axis=1, tiled=True)  13.1 us
    dot_general x5, matrix products, attend(): jnp.einsum('tqhd,tlkhd->tqhlk', query_tiles, key_parts, preferred_element...  12.3 us
    dot_general x5, matrix products, attend(): jnp.einsum('tqhlk,tlkhd->tqhld', weights.astype(jnp.bfloat16), value_part...  11.3 us
    gather x4, local copies, waits for them, and re-layouts, group_pass(): value_group = value_blocks[id_group].reshape(4, -1, heads_dev, head_dim)  8.93 us
    ppermute x6, waiting for transfers between devices, from_behind(): lax.ppermute(x, axis, [(i, (i + by) % devices) for i in range(devices)])  8.04 us
    all_to_all x1, waiting for transfers between devices, shards(): lax.all_to_all(query_parts, 'head', split_axis=1, concat_axis=0, tiled=True)  7.76 us
    all_to_all x1, waiting for transfers between devices, shards(): lax.all_to_all(spread(value_vectors), 'head', split_axis=1, concat_axis=0...  7.61 us
    all_to_all x1, starting transfers between devices, shards(): lax.all_to_all(spread(key_vectors), 'head', split_axis=1, concat_axis=0,...  7.39 us
  transfers between devices with their start and end apart: 9, of which 4 were waited for; matrix products, arithmetic and copies ran while one was open for 47% of the time, Pallas kernels for 0%

commit v1 on v0

--- a/solution.py
+++ b/solution.py
@@ -1,6 +1,10 @@
+import functools
+
 import jax
 import jax.numpy as jnp
 from jax import lax
+from jax.experimental import pallas as pl
+from jax.experimental.pallas import tpu as pltpu
 from jax.sharding import PartitionSpec as P
 
 D = 1024
@@ -188,6 +192,301 @@
     return jnp.dot(restored, out_weight, preferred_element_type=jnp.float32).astype(jnp.bfloat16)
 
 
+HALF = BLK // 2
+PLANE = 4
+
+
+def send_peer(me, step):
+    z, rest = me // PLANE, me % PLANE
+    i, j = step // PLANE, step % PLANE
+    to_z = ((z // 2 + 1 - i // 2) % 2) * 2 + (z + i + i // 2) % 2
+    return to_z * PLANE + (rest + 1 + j) % PLANE
+
+
+def recv_peer(me, step):
+    z, rest = me // PLANE, me % PLANE
+    i, j = step // PLANE, step % PLANE
+    from_z = ((z // 2 + 1 - i // 2) % 2) * 2 + (z + i + i // 2) % 2
+    return from_z * PLANE + (rest + 3 - j) % PLANE
+
+
+def swap_halves(x):
+    return jnp.concatenate([x[:, HALF:], x[:, :HALF]], axis=1)
+
+
+def low_lanes(shape):
+    return lax.broadcasted_iota(jnp.int32, shape, 1) < HALF
+
+
+def fused_kernel(
+    lists, q_ref, k_ref, v_ref, w_hbm, o_ref,
+    kq_out, v_out, kq_near, v_near, k_far, v_far, probs, inv_total, att_out, att_in, w_ref,
+    kq_send, kq_recv, v_send, v_recv, kf_send, kf_recv, vf_send, vf_recv, att_send, att_recv, w_sem,
+):
+    dom = lax.axis_index("dom")
+    me = lax.axis_index("head")
+    other = 1 - dom
+    mesh_id = pl.DeviceIdType.MESH
+
+    barrier = pltpu.get_barrier_semaphore()
+
+    def greet(step, carry):
+        pl.semaphore_signal(
+            barrier, inc=1, device_id=(dom, send_peer(me, step)), device_id_type=mesh_id
+        )
+        return carry
+
+    lax.fori_loop(0, HEADS - 1, greet, 0)
+    pl.semaphore_signal(barrier, inc=1, device_id=(other, me), device_id_type=mesh_id)
+
+    w_copy = pltpu.make_async_copy(w_hbm, w_ref, w_sem)
+    w_copy.start()
+
+    low = low_lanes((HALF, BLK))
+
+    def pack(ref, pair):
+        x = ref[:, pair * BLK : (pair + 1) * BLK]
+        top, bottom = x[:HALF], x[HALF:]
+        return (
+            jnp.where(low, top, swap_halves(bottom)),
+            jnp.where(low, swap_halves(top), bottom),
+        )
+
+    for pair in range(HEADS // 2):
+        for odd, packed in enumerate(pack(k_ref, pair)):
+            kq_out[2 * pair + odd, :HALF, :] = packed
+        for odd, packed in enumerate(pack(q_ref, pair)):
+            kq_out[2 * pair + odd, HALF:, :] = packed * jnp.bfloat16(0.125)
+
+    pl.semaphore_wait(barrier, HEADS)
+
+    def remote(src, dst, send, recv, device):
+        return pltpu.make_async_remote_copy(
+            src_ref=src, dst_ref=dst, send_sem=send, recv_sem=recv,
+            device_id=device, device_id_type=mesh_id,
+        )
+
+    def kq_copy(source, target):
+        return remote(
+            kq_out.at[target], kq_near.at[source], kq_send.at[target], kq_recv.at[source], (dom, target)
+        )
+
+    def v_copy(source, target):
+        return remote(
+            v_out.at[target], v_near.at[source], v_send.at[target], v_recv.at[source], (dom, target)
+        )
+
+    def kf_copy(block):
+        return remote(
+            kq_near.at[block, pl.ds(0, HALF)], k_far.at[block], kf_send.at[block], kf_recv.at[block],
+            (other, me),
+        )
+
+    def vf_copy(block):
+        return remote(
+            v_near.at[block], v_far.at[block], vf_send.at[block], vf_recv.at[block], (other, me)
+        )
+
+    def att_copy(head, block):
+        return remote(
+            att_out.at[block], att_in.at[head], att_send.at[block], att_recv.at[head], (dom, block)
+        )
+
+    def send_kq(step, carry):
+        kq_copy(me, send_peer(me, step)).start()
+        return carry
+
+    lax.fori_loop(0, HEADS - 1, send_kq, 0)
+    kq_near[me] = kq_out[me]
+    kf_copy(me).start()
+
+    for pair in range(HEADS // 2):
+        for odd, packed in enumerate(pack(v_ref, pair)):
+            v_out[2 * pair + odd] = packed
+
+    def send_v(step, carry):
+        v_copy(me, send_peer(me, step)).start()
+        return carry
+
+    lax.fori_loop(0, HEADS - 1, send_v, 0)
+    v_near[me] = v_out[me]
+    vf_copy(me).start()
+
+    def pass_k(step, carry):
+        source = recv_peer(me, step)
+        kq_copy(source, me).wait_recv()
+        kf_copy(source).start()
+        return carry
+
+    lax.fori_loop(0, HEADS - 1, pass_k, 0)
+
+    def await_kf(block, carry):
+        kf_copy(block).wait_recv()
+        return carry
+
+    lax.fori_loop(0, HEADS, await_kf, 0)
+
+    def score_block(block, carry):
+        row = dom * HEADS + block
+        keys = jnp.concatenate(
+            [kq_near[lax.rem(lists[row, c], HEADS), :HALF, :] for c in range(LC)]
+            + [k_far[lax.rem(lists[row, c], HEADS)] for c in range(LC, LC + LE)],
+            axis=0,
+        )
+        packed = kq_near[block, HALF:, :]
+        swapped = swap_halves(packed)
+        zero = jnp.zeros_like(packed)
+        rows = jnp.concatenate(
+            [
+                jnp.where(low, packed, zero),
+                jnp.where(low, swapped, zero),
+                jnp.where(low, zero, swapped),
+                jnp.where(low, zero, packed),
+            ],
+            axis=0,
+        )
+        scores = lax.dot_general(
+            rows, keys, (((1,), (1,)), ((), ())), preferred_element_type=jnp.float32
+        )
+        high = jnp.max(scores, axis=1, keepdims=True)
+        high = jnp.maximum(high[:BLK], high[BLK:])
+        weights = jnp.exp(scores - jnp.concatenate([high, high], axis=0))
+        probs[block] = weights.astype(jnp.bfloat16)
+        total = jnp.sum(weights, axis=1, keepdims=True)
+        inverse = 1.0 / (total[:BLK] + total[BLK:])
+        inv_total[block] = jnp.where(low, inverse[:HALF], inverse[HALF:])
+        return carry
+
+    lax.fori_loop(0, HEADS, score_block, 0)
+
+    def pass_v(step, carry):
+        source = recv_peer(me, step)
+        v_copy(source, me).wait_recv()
+        vf_copy(source).start()
+        return carry
+
+    lax.fori_loop(0, HEADS - 1, pass_v, 0)
+
+    def await_vf(block, carry):
+        vf_copy(block).wait_recv()
+        return carry
+
+    lax.fori_loop(0, HEADS, await_vf, 0)
+
+    def attend_block(block):
+        row = dom * HEADS + block
+        values = jnp.concatenate(
+            [v_near[lax.rem(lists[row, c], HEADS)] for c in range(LC)]
+            + [v_far[lax.rem(lists[row, c], HEADS)] for c in range(LC, LC + LE)],
+            axis=0,
+        )
+        summed = jnp.dot(probs[block], values, preferred_element_type=jnp.float32)
+        first, second = summed[:BLK], summed[BLK:]
+        packed = jnp.where(
+            low,
+            first[:HALF] + swap_halves(second[:HALF]),
+            swap_halves(first[HALF:]) + second[HALF:],
+        )
+        return (packed * inv_total[block]).astype(jnp.bfloat16)
+
+    def attend_and_send(step, carry):
+        block = send_peer(me, step)
+        att_out[block] = attend_block(block)
+        att_copy(me, block).start()
+        return carry
+
+    lax.fori_loop(0, HEADS - 1, attend_and_send, 0)
+    att_in[me] = attend_block(me)
+    w_copy.wait()
+
+    mixed = jnp.zeros((BLK, D), jnp.float32)
+    for i in range(HEADS // PLANE):
+        first_head = (recv_peer(me, i * PLANE) // PLANE) * PLANE
+        for j in range(PLANE):
+            head = first_head + j
+
+            @pl.when(head != me)
+            def _():
+                att_copy(head, me).wait_recv()
+
+        columns = []
+        for j in range(0, PLANE, 2):
+            even, odd = att_in[first_head + j], att_in[first_head + j + 1]
+            columns.append(
+                jnp.concatenate(
+                    [
+                        jnp.where(low, even, swap_halves(odd)),
+                        jnp.where(low, swap_halves(even), odd),
+                    ],
+                    axis=0,
+                )
+            )
+        attended = jnp.concatenate(columns, axis=1)
+        rows_at = pl.multiple_of(first_head * HALF, PLANE * HALF)
+        mixed = mixed + jnp.dot(
+            attended, w_ref[pl.ds(rows_at, PLANE * HALF), :], preferred_element_type=jnp.float32
+        )
+    o_ref[...] = mixed.astype(o_ref.dtype)
+
+    def settle(step, carry):
+        target = send_peer(me, step)
+        kq_copy(me, target).wait_send()
+        v_copy(me, target).wait_send()
+        att_copy(me, target).wait_send()
+        return carry
+
+    lax.fori_loop(0, HEADS - 1, settle, 0)
+
+    def settle_far(block, carry):
+        kf_copy(block).wait_send()
+        vf_copy(block).wait_send()
+        return carry
+
+    lax.fori_loop(0, HEADS, settle_far, 0)
+
+
+def fused_shards(queries, key_vectors, value_vectors, block_lists, out_weight):
+    vmem = pl.BlockSpec(memory_space=pltpu.VMEM)
+    half_blocks = pltpu.VMEM((HEADS, HALF, BLK), jnp.bfloat16)
+    whole_blocks = pltpu.VMEM((HEADS, BLK, BLK), jnp.bfloat16)
+    pairs = HEADS * (LC + LE) * BLK * BLK
+    return pl.pallas_call(
+        fused_kernel,
+        out_shape=jax.ShapeDtypeStruct(queries.shape, jnp.bfloat16),
+        in_specs=[
+            pl.BlockSpec(memory_space=pltpu.SMEM),
+            vmem,
+            vmem,
+            vmem,
+            pl.BlockSpec(memory_space=pl.ANY),
+        ],
+        out_specs=vmem,
+        scratch_shapes=[
+            whole_blocks,
+            half_blocks,
+            whole_blocks,
+            half_blocks,
+            half_blocks,
+            half_blocks,
+            pltpu.VMEM((HEADS, 2 * BLK, (LC + LE) * HALF), jnp.bfloat16),
+            pltpu.VMEM((HEADS, HALF, BLK), jnp.float32),
+            half_blocks,
+            half_blocks,
+            pltpu.VMEM((D, D), jnp.bfloat16),
+        ]
+        + [pltpu.SemaphoreType.DMA((HEADS,))] * 10
+        + [pltpu.SemaphoreType.DMA],
+        compiler_params=pltpu.CompilerParams(
+            collective_id=0, has_side_effects=True, vmem_limit_bytes=48 * 1024 * 1024
+        ),
+        cost_estimate=pl.CostEstimate(
+            flops=4 * pairs * (D // HEADS) + 2 * BLK * D * D,
+            bytes_accessed=4 * BLK * D * 2 + D * D * 2,
+            transcendentals=pairs,
+        ),
+    )(block_lists, queries, key_vectors, value_vectors, out_weight)
+
+
 def solution(mesh):
     in_specs = (
         P(("dom", "head"), None),
@@ -197,4 +496,6 @@
         P(),
     )
     out_specs = P(("dom", "head"), None)
-    return jax.shard_map(shards, mesh=mesh, in_specs=in_specs, out_specs=out_specs, check_vma=False)
+    fused_fits = mesh.shape["dom"] == 2 and mesh.shape["head"] == HEADS
+    body = fused_shards if fused_fits else shards
+    return jax.shard_map(body, mesh=mesh, in_specs=in_specs, out_specs=out_specs, check_vma=False)

time: 139 us -> 59.7 us (0.43)
  Pallas kernels: 0 us -> 53.5 us
  waiting for transfers between devices: 30 us -> 0 us
  local copies, waits for them, and re-layouts: 35.4 us -> 5.92 us
  matrix products: 28.7 us -> 0 us
  starting transfers between devices: 23 us -> 0 us
  blocking collectives: 13.1 us -> 0 us
  other arithmetic: 7.3 us -> 0 us
    pallas_call x0 -> x1, Pallas kernels: none -> 53.5 us  [fused_shards(): pl.pallas_call(fused_kernel, out_shape=jax.ShapeDtypeStruct(queries.shape...]
    dot_general x13 -> x0, matrix products: 28.7 us -> none  [the longest x5 12.3 us: attend(): jnp.einsum('tqhd,tlkhd->tqhlk', query_tiles, key_parts, preferred_element...]
    gather x12 -> x0, local copies, waits for them, and re-layouts: 23.1 us -> none  [the longest x4 8.93 us: group_pass(): value_group = value_blocks[id_group].reshape(4, -1, heads_dev, head_dim)]
    all_to_all x3 -> x0, waiting for transfers between devices: 22 us -> none  [the longest x1 7.76 us: shards(): lax.all_to_all(query_parts, 'head', split_axis=1, concat_axis=0, tiled=True)]
    all_to_all x3 -> x0, starting transfers between devices: 15.8 us -> none  [the longest x1 7.39 us: shards(): lax.all_to_all(spread(key_vectors), 'head', split_axis=1, concat_axis=0,...]
    all_to_all x1 -> x0, blocking collectives: 13.1 us -> none  [shards(): lax.all_to_all(attended, 'head', split_axis=0, concat_axis=1, tiled=True)]
    ppermute x6 -> x0, waiting for transfers between devices: 8.04 us -> none  [from_behind(): lax.ppermute(x, axis, [(i, (i + by) % devices) for i in range(devices)])]
    ppermute x6 -> x0, starting transfers between devices: 7.18 us -> none  [from_behind(): lax.ppermute(x, axis, [(i, (i + by) % devices) for i in range(devices)])]
  transfers between devices with their start and end apart: 9 -> 0, of which waited for: 4 -> 0; matrix products, arithmetic and copies ran while one was open for 47% -> 0% of each run, Pallas kernels for 0% -> 0%
where the time goes in v1:
time: 59.7 us; the launch traced here: 59.4 us
  Pallas kernels  53.5 us (90%)
  local copies, waits for them, and re-layouts  5.92 us (10%)
    pallas_call x1, Pallas kernels, fused_shards(): pl.pallas_call(fused_kernel, out_shape=jax.ShapeDtypeStruct(queries.shape...  53.5 us
    unnamed x10, local copies, waits for them, and re-layouts  5.92 us

profile of v1, /device:TPU:0, one launch (start us, length us, event | category | flops | bytes accessed | tf_op | source)
XLA Modules:
  0.0 59.4 jit_solution(3494650516109315243)
XLA Ops:
  0.0 0.8 %copy.6.lists = s32[32,12]{1,0:T(8,128)S(1)} copy(s32[32,12]{0,1:T(8,128)} %param.8) | data formatting | bytes 3072 | tf_op args[3]
  0.8 0.0 copy-start
  0.8 1.6 %copy-done = bf16[1024,1024]{1,0:T(8,128)(2,1)S(1)} copy-done((bf16[1024,1024]{1,0:T(8,128)(2,1)S(1)}, bf16[1024,1024]{1,0:T(8,128)(2,1)}, u32[]{:S(2)}) %copy-start) | copy-done | bytes 2097176
  2.4 0.0 copy-start.1
  2.4 0.9 %copy-done.1 = bf16[128,1024]{1,0:T(8,128)(2,1)S(1)} copy-done((bf16[128,1024]{1,0:T(8,128)(2,1)S(1)}, bf16[128,1024]{1,0:T(8,128)(2,1)}, u32[]{:S(2)}) %copy-start.1) | copy-done | bytes 262168
  3.3 0.0 copy-start.2
  3.3 0.9 %copy-done.2 = bf16[128,1024]{1,0:T(8,128)(2,1)S(1)} copy-done((bf16[128,1024]{1,0:T(8,128)(2,1)S(1)}, bf16[128,1024]{1,0:T(8,128)(2,1)}, u32[]{:S(2)}) %copy-start.2) | copy-done | bytes 262168
  4.3 0.0 copy-start.3
  4.3 0.9 %copy-done.3 = bf16[128,1024]{1,0:T(8,128)(2,1)S(1)} copy-done((bf16[128,1024]{1,0:T(8,128)(2,1)S(1)}, bf16[128,1024]{1,0:T(8,128)(2,1)}, u32[]{:S(2)}) %copy-start.3) | copy-done | bytes 262168
  5.2 53.5 %shard_map.55 = bf16[128,1024]{1,0:T(8,128)(2,1)S(1)} custom-call(s32[32,12]{1,0:T(8,128)S(1)} %copy.6.lists, bf16[128,1024]{1,0:T(8,128)(2,1)S(1)} %copy-done.1, bf16[128,1024]{1,0:T(8,128)(2,1)S(1)} %copy-done.2, bf16[128,1024]{1,0:T(8,128)(2,1)S(1)} %copy-done.3, bf16[1024,1024]{1,0:T(8,128)(2,1)S(1)} %copy-done), custom_call_target="tpu_custom_call" | custom-call | flops 1073741824 | bytes 3145728 | tf_op jit(solution)/shard_map/pallas_call | solution.py:453
  58.7 0.7 %copy.8 = bf16[128,1024]{1,0:T(8,128)(2,1)} copy(bf16[128,1024]{1,0:T(8,128)(2,1)S(1)} %shard_map.55) | data formatting | bytes 524288
Async XLA Ops:
  0.8 1.6 %copy-start = (bf16[1024,1024]{1,0:T(8,128)(2,1)S(1)}, bf16[1024,1024]{1,0:T(8,128)(2,1)}, u32[]{:S(2)}) copy-start(bf16[1024,1024]{1,0:T(8,128)(2,1)} %w_hbm.1) | copy-start | bytes 6291460
  2.4 0.9 %copy-start.1 = (bf16[128,1024]{1,0:T(8,128)(2,1)S(1)}, bf16[128,1024]{1,0:T(8,128)(2,1)}, u32[]{:S(2)}) copy-start(bf16[128,1024]{1,0:T(8,128)(2,1)} %q_ref.1) | copy-start | bytes 786436
  3.3 0.9 %copy-start.2 = (bf16[128,1024]{1,0:T(8,128)(2,1)S(1)}, bf16[128,1024]{1,0:T(8,128)(2,1)}, u32[]{:S(2)}) copy-start(bf16[128,1024]{1,0:T(8,128)(2,1)} %k_ref.1) | copy-start | bytes 786436
  4.3 0.9 %copy-start.3 = (bf16[128,1024]{1,0:T(8,128)(2,1)S(1)}, bf16[128,1024]{1,0:T(8,128)(2,1)}, u32[]{:S(2)}) copy-start(bf16[128,1024]{1,0:T(8,128)(2,1)} %v_ref.1) | copy-start | bytes 786436

commit v2 on v1

--- a/solution.py
+++ b/solution.py
@@ -219,9 +219,9 @@
 
 
 def fused_kernel(
-    lists, q_ref, k_ref, v_ref, w_hbm, o_ref,
-    kq_out, v_out, kq_near, v_near, k_far, v_far, probs, inv_total, att_out, att_in, w_ref,
-    kq_send, kq_recv, v_send, v_recv, kf_send, kf_recv, vf_send, vf_recv, att_send, att_recv, w_sem,
+    lists, q_hbm, k_hbm, v_hbm, w_hbm, o_ref, q_ref, k_ref, v_ref,
+    k_out, q_out, v_out, k_near, q_near, v_near, k_far, v_far, probs, att_out, att_in, w_ref,
+    in_sem, k_send, k_recv, q_send, q_recv, v_send, v_recv, kf_send, kf_recv, vf_send, vf_recv, att_send, att_recv, w_sem,
 ):
     dom = lax.axis_index("dom")
     me = lax.axis_index("head")
@@ -239,7 +239,13 @@
     lax.fori_loop(0, HEADS - 1, greet, 0)
     pl.semaphore_signal(barrier, inc=1, device_id=(other, me), device_id_type=mesh_id)
 
+    k_load = pltpu.make_async_copy(k_hbm, k_ref, in_sem.at[0])
+    q_load = pltpu.make_async_copy(q_hbm, q_ref, in_sem.at[1])
+    v_load = pltpu.make_async_copy(v_hbm, v_ref, in_sem.at[2])
     w_copy = pltpu.make_async_copy(w_hbm, w_ref, w_sem)
+    k_load.start()
+    q_load.start()
+    v_load.start()
     w_copy.start()
 
     low = low_lanes((HALF, BLK))
@@ -252,12 +258,13 @@
             jnp.where(low, swap_halves(top), bottom),
         )
 
-    for pair in range(HEADS // 2):
-        for odd, packed in enumerate(pack(k_ref, pair)):
-            kq_out[2 * pair + odd, :HALF, :] = packed
-        for odd, packed in enumerate(pack(q_ref, pair)):
-            kq_out[2 * pair + odd, HALF:, :] = packed * jnp.bfloat16(0.125)
-
+    def pack_all(ref, out, factor):
+        for pair in range(HEADS // 2):
+            for odd, packed in enumerate(pack(ref, pair)):
+                out[2 * pair + odd] = packed if factor is None else packed * jnp.bfloat16(factor)
+
+    k_load.wait()
+    pack_all(k_ref, k_out, None)
     pl.semaphore_wait(barrier, HEADS)
 
     def remote(src, dst, send, recv, device):
@@ -266,9 +273,14 @@
             device_id=device, device_id_type=mesh_id,
         )
 
-    def kq_copy(source, target):
+    def k_copy(source, target):
         return remote(
-            kq_out.at[target], kq_near.at[source], kq_send.at[target], kq_recv.at[source], (dom, target)
+            k_out.at[target], k_near.at[source], k_send.at[target], k_recv.at[source], (dom, target)
+        )
+
+    def q_copy(source, target):
+        return remote(
+            q_out.at[target], q_near.at[source], q_send.at[target], q_recv.at[source], (dom, target)
         )
 
     def v_copy(source, target):
@@ -278,8 +290,7 @@
 
     def kf_copy(block):
         return remote(
-            kq_near.at[block, pl.ds(0, HALF)], k_far.at[block], kf_send.at[block], kf_recv.at[block],
-            (other, me),
+            k_near.at[block], k_far.at[block], kf_send.at[block], kf_recv.at[block], (other, me)
         )
 
     def vf_copy(block):
@@ -292,33 +303,37 @@
             att_out.at[block], att_in.at[head], att_send.at[block], att_recv.at[head], (dom, block)
         )
 
-    def send_kq(step, carry):
-        kq_copy(me, send_peer(me, step)).start()
-        return carry
-
-    lax.fori_loop(0, HEADS - 1, send_kq, 0)
-    kq_near[me] = kq_out[me]
+    def send_k(step, carry):
+        k_copy(me, send_peer(me, step)).start()
+        return carry
+
+    lax.fori_loop(0, HEADS - 1, send_k, 0)
+    k_near[me] = k_out[me]
     kf_copy(me).start()
 
-    for pair in range(HEADS // 2):
-        for odd, packed in enumerate(pack(v_ref, pair)):
-            v_out[2 * pair + odd] = packed
-
-    def send_v(step, carry):
-        v_copy(me, send_peer(me, step)).start()
-        return carry
-
-    lax.fori_loop(0, HEADS - 1, send_v, 0)
+    q_load.wait()
+    pack_all(q_ref, q_out, 0.125)
+
+    def send_q(step, carry):
+        q_copy(me, send_peer(me, step)).start()
+        return carry
+
+    lax.fori_loop(0, HEADS - 1, send_q, 0)
+    q_near[me] = q_out[me]
+
+    v_load.wait()
+    pack_all(v_ref, v_out, None)
     v_near[me] = v_out[me]
-    vf_copy(me).start()
 
     def pass_k(step, carry):
         source = recv_peer(me, step)
-        kq_copy(source, me).wait_recv()
+        k_copy(source, me).wait_recv()
         kf_copy(source).start()
+        v_copy(me, send_peer(me, step)).start()
         return carry
 
     lax.fori_loop(0, HEADS - 1, pass_k, 0)
+    vf_copy(me).start()
 
     def await_kf(block, carry):
         kf_copy(block).wait_recv()
@@ -326,14 +341,14 @@
 
     lax.fori_loop(0, HEADS, await_kf, 0)
 
-    def score_block(block, carry):
+    def score_block(block):
         row = dom * HEADS + block
         keys = jnp.concatenate(
-            [kq_near[lax.rem(lists[row, c], HEADS), :HALF, :] for c in range(LC)]
-            + [k_far[lax.rem(lists[row, c], HEADS)] for c in range(LC, LC + LE)],
+            [k_near[lax.rem(lists[c, row], HEADS)] for c in range(LC)]
+            + [k_far[lax.rem(lists[c, row], HEADS)] for c in range(LC, LC + LE)],
             axis=0,
         )
-        packed = kq_near[block, HALF:, :]
+        packed = q_near[block]
         swapped = swap_halves(packed)
         zero = jnp.zeros_like(packed)
         rows = jnp.concatenate(
@@ -348,24 +363,24 @@
         scores = lax.dot_general(
             rows, keys, (((1,), (1,)), ((), ())), preferred_element_type=jnp.float32
         )
-        high = jnp.max(scores, axis=1, keepdims=True)
-        high = jnp.maximum(high[:BLK], high[BLK:])
-        weights = jnp.exp(scores - jnp.concatenate([high, high], axis=0))
-        probs[block] = weights.astype(jnp.bfloat16)
-        total = jnp.sum(weights, axis=1, keepdims=True)
-        inverse = 1.0 / (total[:BLK] + total[BLK:])
-        inv_total[block] = jnp.where(low, inverse[:HALF], inverse[HALF:])
-        return carry
-
-    lax.fori_loop(0, HEADS, score_block, 0)
-
-    def pass_v(step, carry):
+        folded = jnp.maximum(scores[:BLK], scores[BLK:])
+        high = folded[:, :BLK]
+        for at in range(BLK, (LC + LE) * HALF, BLK):
+            high = jnp.maximum(high, folded[:, at : at + BLK])
+        high = jnp.max(high, axis=1, keepdims=True)
+        probs[block, :BLK, :] = jnp.exp(scores[:BLK] - high).astype(jnp.bfloat16)
+        probs[block, BLK:, :] = jnp.exp(scores[BLK:] - high).astype(jnp.bfloat16)
+
+    def score_and_pass(step, carry):
         source = recv_peer(me, step)
+        q_copy(source, me).wait_recv()
+        score_block(source)
         v_copy(source, me).wait_recv()
         vf_copy(source).start()
         return carry
 
-    lax.fori_loop(0, HEADS - 1, pass_v, 0)
+    lax.fori_loop(0, HEADS - 1, score_and_pass, 0)
+    score_block(me)
 
     def await_vf(block, carry):
         vf_copy(block).wait_recv()
@@ -376,18 +391,21 @@
     def attend_block(block):
         row = dom * HEADS + block
         values = jnp.concatenate(
-            [v_near[lax.rem(lists[row, c], HEADS)] for c in range(LC)]
-            + [v_far[lax.rem(lists[row, c], HEADS)] for c in range(LC, LC + LE)],
+            [v_near[lax.rem(lists[c, row], HEADS)] for c in range(LC)]
+            + [v_far[lax.rem(lists[c, row], HEADS)] for c in range(LC, LC + LE)],
             axis=0,
         )
+        values = jnp.concatenate([values, jnp.ones_like(values)], axis=1)
         summed = jnp.dot(probs[block], values, preferred_element_type=jnp.float32)
-        first, second = summed[:BLK], summed[BLK:]
+        first, second = summed[:BLK, :BLK], summed[BLK:, :BLK]
+        total = summed[:BLK, BLK:] + summed[BLK:, BLK:]
+        total = jnp.where(low, total[:HALF], total[HALF:])
         packed = jnp.where(
             low,
             first[:HALF] + swap_halves(second[:HALF]),
             swap_halves(first[HALF:]) + second[HALF:],
         )
-        return (packed * inv_total[block]).astype(jnp.bfloat16)
+        return (packed / total).astype(jnp.bfloat16)
 
     def attend_and_send(step, carry):
         block = send_peer(me, step)
@@ -430,7 +448,8 @@
 
     def settle(step, carry):
         target = send_peer(me, step)
-        kq_copy(me, target).wait_send()
+        k_copy(me, target).wait_send()
+        q_copy(me, target).wait_send()
         v_copy(me, target).wait_send()
         att_copy(me, target).wait_send()
         return carry
@@ -447,44 +466,40 @@
 
 def fused_shards(queries, key_vectors, value_vectors, block_lists, out_weight):
     vmem = pl.BlockSpec(memory_space=pltpu.VMEM)
+    hbm = pl.BlockSpec(memory_space=pl.ANY)
     half_blocks = pltpu.VMEM((HEADS, HALF, BLK), jnp.bfloat16)
-    whole_blocks = pltpu.VMEM((HEADS, BLK, BLK), jnp.bfloat16)
     pairs = HEADS * (LC + LE) * BLK * BLK
     return pl.pallas_call(
         fused_kernel,
         out_shape=jax.ShapeDtypeStruct(queries.shape, jnp.bfloat16),
         in_specs=[
             pl.BlockSpec(memory_space=pltpu.SMEM),
-            vmem,
-            vmem,
-            vmem,
-            pl.BlockSpec(memory_space=pl.ANY),
+            hbm,
+            hbm,
+            hbm,
+            hbm,
         ],
         out_specs=vmem,
-        scratch_shapes=[
-            whole_blocks,
-            half_blocks,
-            whole_blocks,
-            half_blocks,
-            half_blocks,
-            half_blocks,
+        scratch_shapes=[pltpu.VMEM((BLK, D), jnp.bfloat16)] * 3
+        + [half_blocks] * 8
+        + [
             pltpu.VMEM((HEADS, 2 * BLK, (LC + LE) * HALF), jnp.bfloat16),
-            pltpu.VMEM((HEADS, HALF, BLK), jnp.float32),
             half_blocks,
             half_blocks,
             pltpu.VMEM((D, D), jnp.bfloat16),
+            pltpu.SemaphoreType.DMA((3,)),
         ]
-        + [pltpu.SemaphoreType.DMA((HEADS,))] * 10
+        + [pltpu.SemaphoreType.DMA((HEADS,))] * 12
         + [pltpu.SemaphoreType.DMA],
         compiler_params=pltpu.CompilerParams(
-            collective_id=0, has_side_effects=True, vmem_limit_bytes=48 * 1024 * 1024
+            collective_id=0, has_side_effects=True, vmem_limit_bytes=60 * 1024 * 1024
         ),
         cost_estimate=pl.CostEstimate(
             flops=4 * pairs * (D // HEADS) + 2 * BLK * D * D,
             bytes_accessed=4 * BLK * D * 2 + D * D * 2,
             transcendentals=pairs,
         ),
-    )(block_lists, queries, key_vectors, value_vectors, out_weight)
+    )(block_lists.T, queries, key_vectors, value_vectors, out_weight)
 
 
 def solution(mesh):

time: 59.7 us -> 46.6 us (0.78)
  Pallas kernels: 53.5 us -> 44.8 us
  local copies, waits for them, and re-layouts: 5.92 us -> 1.67 us
    pallas_call x1, Pallas kernels: 53.5 us -> 44.8 us  [fused_shards(): pl.pallas_call(fused_kernel, out_shape=jax.ShapeDtypeStruct(queries.shape...]
    unnamed x10 -> x1, local copies, waits for them, and re-layouts: 5.92 us -> 1.67 us
where the time goes in v2:
time: 46.6 us; the launch traced here: 46.4 us
  Pallas kernels  44.8 us (96%)
  local copies, waits for them, and re-layouts  1.67 us (4%)
    pallas_call x1, Pallas kernels, fused_shards(): pl.pallas_call(fused_kernel, out_shape=jax.ShapeDtypeStruct(queries.shape...  44.8 us
    unnamed x1, local copies, waits for them, and re-layouts  1.67 us

profile of v2, /device:TPU:0, one launch (start us, length us, event | category | flops | bytes accessed | tf_op | source)
XLA Modules:
  0.0 46.4 jit_solution(12121486447012956232)
XLA Ops:
  0.0 44.8 %shard_map.55 = bf16[128,1024]{1,0:T(8,128)(2,1)} custom-call(s32[12,32]{1,0:T(8,128)} %bitcast.1, bf16[128,1024]{1,0:T(8,128)(2,1)} %q_hbm.1, bf16[128,1024]{1,0:T(8,128)(2,1)} %k_hbm.1, bf16[128,1024]{1,0:T(8,128)(2,1)} %v_hbm.1, bf16[1024,1024]{1,0:T(8,128)(2,1)} %w_hbm.1), custom_call_target="tpu_custom_call" | custom-call | flops 1073741824 | bytes 3145728 | tf_op jit(solution)/shard_map/pallas_call | solution.py:472
  44.8 1.7 %copy.7 = bf16[128,1024]{1,0:T(8,128)(2,1)} copy(bf16[128,1024]{1,0:T(8,128)(2,1)} %shard_map.55) | data formatting | bytes 524288

commit v3 on v2

--- a/solution.py
+++ b/solution.py
@@ -196,18 +196,20 @@
 PLANE = 4
 
 
+def plane_at(me, turn):
+    z = me // PLANE
+    return ((z // 2 + 1 - turn // 2) % 2) * 2 + (z + turn + turn // 2) % 2
+
+
 def send_peer(me, step):
-    z, rest = me // PLANE, me % PLANE
-    i, j = step // PLANE, step % PLANE
-    to_z = ((z // 2 + 1 - i // 2) % 2) * 2 + (z + i + i // 2) % 2
-    return to_z * PLANE + (rest + 1 + j) % PLANE
+    turn, place = step // PLANE, step % PLANE
+    return plane_at(me, turn) * PLANE + (me % PLANE + 1 + place) % PLANE
 
 
 def recv_peer(me, step):
-    z, rest = me // PLANE, me % PLANE
-    i, j = step // PLANE, step % PLANE
-    from_z = ((z // 2 + 1 - i // 2) % 2) * 2 + (z + i + i // 2) % 2
-    return from_z * PLANE + (rest + 3 - j) % PLANE
+    step = HEADS - 2 - step
+    turn, place = step // PLANE, step % PLANE
+    return plane_at(me, turn) * PLANE + (me % PLANE + 3 - place) % PLANE
 
 
 def swap_halves(x):
@@ -236,7 +238,8 @@
         )
         return carry
 
-    lax.fori_loop(0, HEADS - 1, greet, 0)
+    for step in range(HEADS - 1):
+        greet(step, 0)
     pl.semaphore_signal(barrier, inc=1, device_id=(other, me), device_id_type=mesh_id)
 
     k_load = pltpu.make_async_copy(k_hbm, k_ref, in_sem.at[0])
@@ -325,11 +328,16 @@
     pack_all(v_ref, v_out, None)
     v_near[me] = v_out[me]
 
+    def send_v(step, carry):
+        v_copy(me, send_peer(me, step)).start()
+        return carry
+
+    lax.fori_loop(0, HEADS - 1, send_v, 0)
+
     def pass_k(step, carry):
         source = recv_peer(me, step)
         k_copy(source, me).wait_recv()
         kf_copy(source).start()
-        v_copy(me, send_peer(me, step)).start()
         return carry
 
     lax.fori_loop(0, HEADS - 1, pass_k, 0)
@@ -419,7 +427,7 @@
 
     mixed = jnp.zeros((BLK, D), jnp.float32)
     for i in range(HEADS // PLANE):
-        first_head = (recv_peer(me, i * PLANE) // PLANE) * PLANE
+        first_head = plane_at(me, i) * PLANE
         for j in range(PLANE):
             head = first_head + j
 

time: 46.6 us -> 44.2 us (0.948)
  Pallas kernels: 44.8 us -> 42.3 us
    pallas_call x1, Pallas kernels: 44.8 us -> 42.3 us  [fused_shards(): pl.pallas_call(fused_kernel, out_shape=jax.ShapeDtypeStruct(queries.shape...]
where the time goes in v3:
time: 44.2 us; the launch traced here: 44 us
  Pallas kernels  42.3 us (96%)
  local copies, waits for them, and re-layouts  1.67 us (4%)
    pallas_call x1, Pallas kernels, fused_shards(): pl.pallas_call(fused_kernel, out_shape=jax.ShapeDtypeStruct(queries.shape...  42.3 us
    unnamed x1, local copies, waits for them, and re-layouts  1.67 us

profile of v3, /device:TPU:0, one launch (start us, length us, event | category | flops | bytes accessed | tf_op | source)
XLA Modules:
  0.0 44.0 jit_solution(442331000015455840)
XLA Ops:
  0.0 42.3 %shard_map.55 = bf16[128,1024]{1,0:T(8,128)(2,1)} custom-call(s32[12,32]{1,0:T(8,128)} %bitcast.1, bf16[128,1024]{1,0:T(8,128)(2,1)} %q_hbm.1, bf16[128,1024]{1,0:T(8,128)(2,1)} %k_hbm.1, bf16[128,1024]{1,0:T(8,128)(2,1)} %v_hbm.1, bf16[1024,1024]{1,0:T(8,128)(2,1)} %w_hbm.1), custom_call_target="tpu_custom_call" | custom-call | flops 1073741824 | bytes 3145728 | tf_op jit(solution)/shard_map/pallas_call | solution.py:480
  42.3 1.7 %copy.7 = bf16[128,1024]{1,0:T(8,128)(2,1)} copy(bf16[128,1024]{1,0:T(8,128)(2,1)} %shard_map.55) | data formatting | bytes 524288

commit v4 on v3

--- a/solution.py
+++ b/solution.py
@@ -196,20 +196,20 @@
 PLANE = 4
 
 
-def plane_at(me, turn):
-    z = me // PLANE
-    return ((z // 2 + 1 - turn // 2) % 2) * 2 + (z + turn + turn // 2) % 2
+def chip_at(me, turn, place):
+    x, z, y = me // 8, (me // 2) % 4, me % 2
+    to_z = ((z // 2 + 1 - turn // 2) % 2) * 2 + (z + turn + turn // 2) % 2
+    spot = (x * 2 + y + place) % PLANE
+    return (spot // 2) * 8 + to_z * 2 + spot % 2
 
 
 def send_peer(me, step):
-    turn, place = step // PLANE, step % PLANE
-    return plane_at(me, turn) * PLANE + (me % PLANE + 1 + place) % PLANE
+    return chip_at(me, step // PLANE, 1 + step % PLANE)
 
 
 def recv_peer(me, step):
     step = HEADS - 2 - step
-    turn, place = step // PLANE, step % PLANE
-    return plane_at(me, turn) * PLANE + (me % PLANE + 3 - place) % PLANE
+    return chip_at(me, step // PLANE, 3 - step % PLANE)
 
 
 def swap_halves(x):
@@ -222,25 +222,32 @@
 
 def fused_kernel(
     lists, q_hbm, k_hbm, v_hbm, w_hbm, o_ref, q_ref, k_ref, v_ref,
-    k_out, q_out, v_out, k_near, q_near, v_near, k_far, v_far, probs, att_out, att_in, w_ref,
+    k_out, q_out, v_out, q_near, k_all, v_all, probs, att_out, att_in, w_ref,
     in_sem, k_send, k_recv, q_send, q_recv, v_send, v_recv, kf_send, kf_recv, vf_send, vf_recv, att_send, att_recv, w_sem,
 ):
-    dom = lax.axis_index("dom")
-    me = lax.axis_index("head")
-    other = 1 - dom
+    core = lax.axis_index("head") % 2
+    me = lax.axis_index("dom") * 8 + lax.axis_index("head") // 2
+
+    def device(chip, on_core):
+        return (chip // 8, (chip % 8) * 2 + on_core)
+
+    def mine(chip):
+        return chip * 2 + core
+
+    sibling = device(me, 1 - core)
     mesh_id = pl.DeviceIdType.MESH
 
     barrier = pltpu.get_barrier_semaphore()
 
     def greet(step, carry):
         pl.semaphore_signal(
-            barrier, inc=1, device_id=(dom, send_peer(me, step)), device_id_type=mesh_id
+            barrier, inc=1, device_id=device(send_peer(me, step), core), device_id_type=mesh_id
         )
         return carry
 
     for step in range(HEADS - 1):
         greet(step, 0)
-    pl.semaphore_signal(barrier, inc=1, device_id=(other, me), device_id_type=mesh_id)
+    pl.semaphore_signal(barrier, inc=1, device_id=sibling, device_id_type=mesh_id)
 
     k_load = pltpu.make_async_copy(k_hbm, k_ref, in_sem.at[0])
     q_load = pltpu.make_async_copy(q_hbm, q_ref, in_sem.at[1])
@@ -270,40 +277,46 @@
     pack_all(k_ref, k_out, None)
     pl.semaphore_wait(barrier, HEADS)
 
-    def remote(src, dst, send, recv, device):
+    def remote(src, dst, send, recv, target):
         return pltpu.make_async_remote_copy(
             src_ref=src, dst_ref=dst, send_sem=send, recv_sem=recv,
-            device_id=device, device_id_type=mesh_id,
+            device_id=target, device_id_type=mesh_id,
         )
 
     def k_copy(source, target):
         return remote(
-            k_out.at[target], k_near.at[source], k_send.at[target], k_recv.at[source], (dom, target)
+            k_out.at[target], k_all.at[mine(source)], k_send.at[target], k_recv.at[source],
+            device(target, core),
         )
 
     def q_copy(source, target):
         return remote(
-            q_out.at[target], q_near.at[source], q_send.at[target], q_recv.at[source], (dom, target)
+            q_out.at[target], q_near.at[source], q_send.at[target], q_recv.at[source],
+            device(target, core),
         )
 
     def v_copy(source, target):
         return remote(
-            v_out.at[target], v_near.at[source], v_send.at[target], v_recv.at[source], (dom, target)
-        )
-
-    def kf_copy(block):
+            v_out.at[target], v_all.at[mine(source)], v_send.at[target], v_recv.at[source],
+            device(target, core),
+        )
+
+    def kf_copy(chip, on_core):
+        block = chip * 2 + on_core
         return remote(
-            k_near.at[block], k_far.at[block], kf_send.at[block], kf_recv.at[block], (other, me)
-        )
-
-    def vf_copy(block):
+            k_all.at[block], k_all.at[block], kf_send.at[chip], kf_recv.at[chip], sibling
+        )
+
+    def vf_copy(chip, on_core):
+        block = chip * 2 + on_core
         return remote(
-            v_near.at[block], v_far.at[block], vf_send.at[block], vf_recv.at[block], (other, me)
-        )
-
-    def att_copy(head, block):
+            v_all.at[block], v_all.at[block], vf_send.at[chip], vf_recv.at[chip], sibling
+        )
+
+    def att_copy(head, target):
         return remote(
-            att_out.at[block], att_in.at[head], att_send.at[block], att_recv.at[head], (dom, block)
+            att_out.at[target], att_in.at[head], att_send.at[target], att_recv.at[head],
+            device(target, core),
         )
 
     def send_k(step, carry):
@@ -311,8 +324,8 @@
         return carry
 
     lax.fori_loop(0, HEADS - 1, send_k, 0)
-    k_near[me] = k_out[me]
-    kf_copy(me).start()
+    k_all[mine(me)] = k_out[me]
+    kf_copy(me, core).start()
 
     q_load.wait()
     pack_all(q_ref, q_out, 0.125)
@@ -326,7 +339,7 @@
 
     v_load.wait()
     pack_all(v_ref, v_out, None)
-    v_near[me] = v_out[me]
+    v_all[mine(me)] = v_out[me]
 
     def send_v(step, carry):
         v_copy(me, send_peer(me, step)).start()
@@ -337,24 +350,22 @@
     def pass_k(step, carry):
         source = recv_peer(me, step)
         k_copy(source, me).wait_recv()
-        kf_copy(source).start()
+        kf_copy(source, core).start()
         return carry
 
     lax.fori_loop(0, HEADS - 1, pass_k, 0)
-    vf_copy(me).start()
+    vf_copy(me, core).start()
 
     def await_kf(block, carry):
-        kf_copy(block).wait_recv()
+        kf_copy(block, 1 - core).wait_recv()
         return carry
 
     lax.fori_loop(0, HEADS, await_kf, 0)
 
     def score_block(block):
-        row = dom * HEADS + block
+        row = mine(block)
         keys = jnp.concatenate(
-            [k_near[lax.rem(lists[c, row], HEADS)] for c in range(LC)]
-            + [k_far[lax.rem(lists[c, row], HEADS)] for c in range(LC, LC + LE)],
-            axis=0,
+            [k_all[lists[c, row]] for c in range(LC + LE)], axis=0
         )
         packed = q_near[block]
         swapped = swap_halves(packed)
@@ -384,24 +395,22 @@
         q_copy(source, me).wait_recv()
         score_block(source)
         v_copy(source, me).wait_recv()
-        vf_copy(source).start()
+        vf_copy(source, core).start()
         return carry
 
     lax.fori_loop(0, HEADS - 1, score_and_pass, 0)
     score_block(me)
 
     def await_vf(block, carry):
-        vf_copy(block).wait_recv()
+        vf_copy(block, 1 - core).wait_recv()
         return carry
 
     lax.fori_loop(0, HEADS, await_vf, 0)
 
     def attend_block(block):
-        row = dom * HEADS + block
+        row = mine(block)
         values = jnp.concatenate(
-            [v_near[lax.rem(lists[c, row], HEADS)] for c in range(LC)]
-            + [v_far[lax.rem(lists[c, row], HEADS)] for c in range(LC, LC + LE)],
-            axis=0,
+            [v_all[lists[c, row]] for c in range(LC + LE)], axis=0
         )
         values = jnp.concatenate([values, jnp.ones_like(values)], axis=1)
         summed = jnp.dot(probs[block], values, preferred_element_type=jnp.float32)
@@ -426,18 +435,17 @@
     w_copy.wait()
 
     mixed = jnp.zeros((BLK, D), jnp.float32)
-    for i in range(HEADS // PLANE):
-        first_head = plane_at(me, i) * PLANE
-        for j in range(PLANE):
-            head = first_head + j
-
-            @pl.when(head != me)
-            def _():
-                att_copy(head, me).wait_recv()
-
-        columns = []
-        for j in range(0, PLANE, 2):
-            even, odd = att_in[first_head + j], att_in[first_head + j + 1]
+    for turn in range(HEADS // PLANE):
+        columns, weight_rows = [], []
+        for x in range(2):
+            first = (chip_at(me, turn, 0) // 2 % 4) * 2 + x * 8
+            for head in (first, first + 1):
+
+                @pl.when(head != me)
+                def _():
+                    att_copy(head, me).wait_recv()
+
+            even, odd = att_in[first], att_in[first + 1]
             columns.append(
                 jnp.concatenate(
                     [
@@ -447,10 +455,12 @@
                     axis=0,
                 )
             )
-        attended = jnp.concatenate(columns, axis=1)
-        rows_at = pl.multiple_of(first_head * HALF, PLANE * HALF)
+            rows_at = pl.multiple_of(first * HALF, BLK)
+            weight_rows.append(w_ref[pl.ds(rows_at, BLK), :])
         mixed = mixed + jnp.dot(
-            attended, w_ref[pl.ds(rows_at, PLANE * HALF), :], preferred_element_type=jnp.float32
+            jnp.concatenate(columns, axis=1),
+            jnp.concatenate(weight_rows, axis=0),
+            preferred_element_type=jnp.float32,
         )
     o_ref[...] = mixed.astype(o_ref.dtype)
 
@@ -465,8 +475,8 @@
     lax.fori_loop(0, HEADS - 1, settle, 0)
 
     def settle_far(block, carry):
-        kf_copy(block).wait_send()
-        vf_copy(block).wait_send()
+        kf_copy(block, core).wait_send()
+        vf_copy(block, core).wait_send()
         return carry
 
     lax.fori_loop(0, HEADS, settle_far, 0)
@@ -489,7 +499,8 @@
         ],
         out_specs=vmem,
         scratch_shapes=[pltpu.VMEM((BLK, D), jnp.bfloat16)] * 3
-        + [half_blocks] * 8
+        + [half_blocks] * 4
+        + [pltpu.VMEM((2 * HEADS, HALF, BLK), jnp.bfloat16)] * 2
         + [
             pltpu.VMEM((HEADS, 2 * BLK, (LC + LE) * HALF), jnp.bfloat16),
             half_blocks,

time: 44.2 us -> 42.6 us (0.964)
  Pallas kernels: 42.3 us -> 40.7 us
    pallas_call x1, Pallas kernels: 42.3 us -> 40.7 us  [fused_shards(): pl.pallas_call(fused_kernel, out_shape=jax.ShapeDtypeStruct(queries.shape...]
where the time goes in v4:
time: 42.6 us; the launch traced here: 42.4 us
  Pallas kernels  40.7 us (96%)
  local copies, waits for them, and re-layouts  1.67 us (4%)
    pallas_call x1, Pallas kernels, fused_shards(): pl.pallas_call(fused_kernel, out_shape=jax.ShapeDtypeStruct(queries.shape...  40.7 us
    unnamed x1, local copies, waits for them, and re-layouts  1.67 us

profile of v4, /device:TPU:0, one launch (start us, length us, event | category | flops | bytes accessed | tf_op | source)
XLA Modules:
  0.0 42.4 jit_solution(13085271092490795255)
XLA Ops:
  0.0 40.7 %shard_map.55 = bf16[128,1024]{1,0:T(8,128)(2,1)} custom-call(s32[12,32]{1,0:T(8,128)} %bitcast.1, bf16[128,1024]{1,0:T(8,128)(2,1)} %q_hbm.1, bf16[128,1024]{1,0:T(8,128)(2,1)} %k_hbm.1, bf16[128,1024]{1,0:T(8,128)(2,1)} %v_hbm.1, bf16[1024,1024]{1,0:T(8,128)(2,1)} %w_hbm.1), custom_call_target="tpu_custom_call" | custom-call | flops 1073741824 | bytes 3145728 | tf_op jit(solution)/shard_map/pallas_call | solution.py:490
  40.8 1.7 %copy.7 = bf16[128,1024]{1,0:T(8,128)(2,1)} copy(bf16[128,1024]{1,0:T(8,128)(2,1)} %shard_map.55) | data formatting | bytes 524288

commit v5 on v4

--- a/solution.py
+++ b/solution.py
@@ -323,7 +323,8 @@
         k_copy(me, send_peer(me, step)).start()
         return carry
 
-    lax.fori_loop(0, HEADS - 1, send_k, 0)
+    for step in range(HEADS - 1):
+        send_k(step, 0)
     k_all[mine(me)] = k_out[me]
     kf_copy(me, core).start()
 
@@ -334,7 +335,8 @@
         q_copy(me, send_peer(me, step)).start()
         return carry
 
-    lax.fori_loop(0, HEADS - 1, send_q, 0)
+    for step in range(HEADS - 1):
+        send_q(step, 0)
     q_near[me] = q_out[me]
 
     v_load.wait()
@@ -345,7 +347,8 @@
         v_copy(me, send_peer(me, step)).start()
         return carry
 
-    lax.fori_loop(0, HEADS - 1, send_v, 0)
+    for step in range(HEADS - 1):
+        send_v(step, 0)
 
     def pass_k(step, carry):
         source = recv_peer(me, step)
@@ -433,6 +436,22 @@
     lax.fori_loop(0, HEADS - 1, attend_and_send, 0)
     att_in[me] = attend_block(me)
     w_copy.wait()
+
+    def settle(step, carry):
+        target = send_peer(me, step)
+        k_copy(me, target).wait_send()
+        q_copy(me, target).wait_send()
+        v_copy(me, target).wait_send()
+        return carry
+
+    lax.fori_loop(0, HEADS - 1, settle, 0)
+
+    def settle_far(block, carry):
+        kf_copy(block, core).wait_send()
+        vf_copy(block, core).wait_send()
+        return carry
+
+    lax.fori_loop(0, HEADS, settle_far, 0)
 
     mixed = jnp.zeros((BLK, D), jnp.float32)
     for turn in range(HEADS // PLANE):
@@ -462,24 +481,16 @@
             jnp.concatenate(weight_rows, axis=0),
             preferred_element_type=jnp.float32,
         )
-    o_ref[...] = mixed.astype(o_ref.dtype)
-
-    def settle(step, carry):
-        target = send_peer(me, step)
-        k_copy(me, target).wait_send()
-        q_copy(me, target).wait_send()
-        v_copy(me, target).wait_send()
-        att_copy(me, target).wait_send()
-        return carry
-
-    lax.fori_loop(0, HEADS - 1, settle, 0)
-
-    def settle_far(block, carry):
-        kf_copy(block, core).wait_send()
-        vf_copy(block, core).wait_send()
-        return carry
-
-    lax.fori_loop(0, HEADS, settle_far, 0)
+    q_ref[...] = mixed.astype(q_ref.dtype)
+    o_copy = pltpu.make_async_copy(q_ref, o_ref, in_sem.at[0])
+    o_copy.start()
+
+    def settle_att(step, carry):
+        att_copy(me, send_peer(me, step)).wait_send()
+        return carry
+
+    lax.fori_loop(0, HEADS - 1, settle_att, 0)
+    o_copy.wait()
 
 
 def fused_shards(queries, key_vectors, value_vectors, block_lists, out_weight):
@@ -497,7 +508,7 @@
             hbm,
             hbm,
         ],
-        out_specs=vmem,
+        out_specs=hbm,
         scratch_shapes=[pltpu.VMEM((BLK, D), jnp.bfloat16)] * 3
         + [half_blocks] * 4
         + [pltpu.VMEM((2 * HEADS, HALF, BLK), jnp.bfloat16)] * 2

time: 42.6 us -> 41.9 us (0.984)
  Pallas kernels: 40.7 us -> 40.1 us
    pallas_call x1, Pallas kernels: 40.7 us -> 40.1 us  [fused_shards(): pl.pallas_call(fused_kernel, out_shape=jax.ShapeDtypeStruct(queries.shape...]
where the time goes in v5:
time: 41.9 us; the launch traced here: 41.7 us
  Pallas kernels  40.1 us (96%)
  local copies, waits for them, and re-layouts  1.67 us (4%)
    pallas_call x1, Pallas kernels, fused_shards(): pl.pallas_call(fused_kernel, out_shape=jax.ShapeDtypeStruct(queries.shape...  40.1 us
    unnamed x1, local copies, waits for them, and re-layouts  1.67 us

profile of v5, /device:TPU:0, one launch (start us, length us, event | category | flops | bytes accessed | tf_op | source)
XLA Modules:
  0.0 41.7 jit_solution(4246702517528202459)
XLA Ops:
  0.0 40.1 %shard_map.55 = bf16[128,1024]{1,0:T(8,128)(2,1)} custom-call(s32[12,32]{1,0:T(8,128)} %bitcast.1, bf16[128,1024]{1,0:T(8,128)(2,1)} %q_hbm.1, bf16[128,1024]{1,0:T(8,128)(2,1)} %k_hbm.1, bf16[128,1024]{1,0:T(8,128)(2,1)} %v_hbm.1, bf16[1024,1024]{1,0:T(8,128)(2,1)} %w_hbm.1), custom_call_target="tpu_custom_call" | custom-call | flops 1073741824 | bytes 3145728 | tf_op jit(solution)/shard_map/pallas_call | solution.py:501
  40.1 1.7 %copy.7 = bf16[128,1024]{1,0:T(8,128)(2,1)} copy(bf16[128,1024]{1,0:T(8,128)(2,1)} %shard_map.55) | data formatting | bytes 524288
